TPU v7x, 128 devices: a whole 4x4x4 slice. The times are simulated.
128 devices in a mesh: blk: 8 (over x, z_lo), bcast: 16 (over z_hi, y, core).
Axes of the slice: x: 4, y: 4, z: 4 (z_hi: 2, z_lo: 2; z = z_hi * 2 + z_lo), core: 2. Of those that a mesh axis runs over, the one named last changes fastest.
Arguments:
- coupling: float32 [8192, 4096], P('blk', 'bcast'), may hold values from -6 to 6
- denominators: float32 [8192, 4096], P('blk', 'bcast'), may hold values from 1.5 to 6
- integrals: bfloat16 [4096, 4096], P('bcast', 'blk'), may hold values from -0.125 to 0.125
- tile_sizes: int32 [32], replicated, may hold values from 64 to 128, as said below
- screen_ov: int32 [64, 32], replicated, may hold values 0 or 1
- screen_vv: int32 [32, 32], replicated, may hold values 0 or 1
Outputs:
- amplitudes: float32 [8192, 4096], P('blk', 'bcast')
Inputs may be any that keep to these rules, and one draw needn't show every extreme that they name: `tile_sizes`: each pair tile has between 64 and 128 live pairs; some tile has exactly 128 and some exactly 64.
All inputs are finite; a program needn't handle non-finite values.
Results may differ from a plain program's by a relative error of at most 0.0012.
Values may be sent and summed in bfloat16 or wider, within the bound.
A program may use at most 64 MiB of HBM per device.

v0:
```python
import jax
import jax.numpy as jnp
from jax import lax
from jax.sharding import PartitionSpec as P

TILE = 128
ROW_TILE = 128
ITERS = 3


def local(coupling, denominators, integrals, tile_sizes, screen_ov, screen_vv):
    blk_id = lax.axis_index("blk")
    grp_id = lax.axis_index("bcast")
    rows, cols = coupling.shape
    own_tiles = cols // TILE
    row_tiles = rows // ROW_TILE
    group = integrals.shape[1]
    group_tiles = group // TILE
    sizes_here = lax.dynamic_slice_in_dim(tile_sizes, grp_id * own_tiles, own_tiles)
    ov_here = lax.dynamic_slice(
        screen_ov, (blk_id * row_tiles, grp_id * own_tiles), (row_tiles, own_tiles)
    )
    live = (jnp.arange(TILE)[None, :] < sizes_here[:, None]).astype(jnp.float32)
    block = ov_here.astype(jnp.float32)[:, None, :, None] * live[None, None, :, :]
    keep = jnp.broadcast_to(block, (row_tiles, ROW_TILE, own_tiles, TILE)).reshape(rows, cols)
    vv_here = lax.dynamic_slice(
        screen_vv, (grp_id * own_tiles, blk_id * group_tiles), (own_tiles, group_tiles)
    )
    screened = (
        integrals.reshape(own_tiles, TILE, group_tiles, TILE)
        * vv_here.astype(jnp.bfloat16)[:, None, :, None]
    ).reshape(cols, group)
    amplitudes = coupling * keep / denominators
    for step in range(ITERS):
        rounded = amplitudes.astype(jnp.bfloat16)
        gathered = lax.all_gather(rounded, "bcast", axis=1, tiled=True)
        ladder = lax.dot_general(
            gathered,
            lax.all_gather(screened, "blk", axis=1, tiled=True),
            (((1,), (1,)), ((), ())),
            preferred_element_type=jnp.float32,
        )
        amplitudes = (coupling + ladder) * keep / denominators
    return amplitudes


def solution(mesh):
    in_specs = (P("blk", "bcast"), P("blk", "bcast"), P("bcast", "blk"), P(), P(), P())
    out_specs = P("blk", "bcast")
    return jax.shard_map(local, mesh=mesh, in_specs=in_specs, out_specs=out_specs, check_vma=False)
```

profile of v0, /device:TPU:0, one launch (start us, length us, event | category | flops | bytes accessed | tf_op | source)
XLA Modules:
  0.0 331.9 jit_solution(826627992025669431)
XLA Ops:
  6.5 0.0 all-gather.7.cloned.1.call-start
  6.5 0.8 dynamic-slice_convert_fusion
  7.3 0.1 mul.59
  7.4 1.7 bitcast_multiply_fusion.1
  9.2 0.0 all-gather.7.cloned.1.call-update
  9.2 0.0 all-gather.5.cloned.1.call-start
  9.2 0.7 dynamic_slice.10
  10.0 0.8 dynamic-slice_convert_fusion.1
  10.7 0.1 copy.7
  10.8 0.1 compare_convert_fusion
  10.9 0.1 broadcast_multiply_fusion
  11.0 0.3 broadcast_in_dim.2
  11.2 2.6 fusion.9
  13.8 0.0 all-gather.5.cloned.1.call-update
  13.8 0.0 copy-start
  13.8 0.0 copy-start.1
  13.8 0.0 all-gather.9.cloned.1.call-start
  13.9 49.1 %all-gather.7.cloned.1.call-done = bf16[256,4096]{1,0:T(8,128)(2,1)} async-done(((bf16[256,512]{1,0:T(8,128)(2,1)}), bf16[256,4096]{1,0:T(8,128)(2,1)}) %all-gather.7.cloned.1.call-update) | async-done | bytes 2097168 | tf_op jit(solution)/shard_map/all_gather | solution.py:39
  63.0 82.7 %all-gather.5.cloned.1.call-done = bf16[1024,4096]{1,0:T(8,128)(2,1)} async-done(((bf16[1024,256]{1,0:T(8,128)(2,1)}), bf16[1024,4096]{1,0:T(8,128)(2,1)}) %all-gather.5.cloned.1.call-update) | async-done | bytes 8388624 | tf_op jit(solution)/shard_map/all_gather | solution.py:36
  145.8 7.7 %fusion.4 = bf16[1024,256]{1,0:T(8,128)(2,1)} fusion(f32[1024,256]{1,0:T(8,128)} %param.7, f32[1024,256]{1,0:T(8,128)} %param.6, bf16[1024,4096]{1,0:T(8,128)(2,1)} %all-gather.5.cloned.1.call-done, bf16[256,4096]{1,0:T(8,128)(2,1)} %all-gather.7.cloned.1.call-done, f32[128,8,2,128]{3,2,1,0:T(2,128)S(1)} %bitcast.22), kind=kOutput, calls=%fused_computation.7 | convolution fusion | flops 2148532224 | bytes 14155776 | tf_op jit(solution)/shard_map/dot_general | solution.py:37
  153.5 0.0 all-gather.9.cloned.1.call-update
  153.5 0.0 all-gather.11.cloned.1.call-start
  153.6 78.6 %all-gather.9.cloned.1.call-done = bf16[1024,4096]{1,0:T(8,128)(2,1)} async-done(((bf16[1024,256]{1,0:T(8,128)(2,1)}), bf16[1024,4096]{1,0:T(8,128)(2,1)}) %all-gather.9.cloned.1.call-update) | async-done | bytes 8388624 | tf_op jit(solution)/shard_map/all_gather | solution.py:36
  232.2 0.0 copy-done
  232.2 0.0 copy-done.1
  232.2 7.1 %fusion.6 = bf16[1024,256]{1,0:T(8,128)(2,1)} fusion(f32[1024,256]{1,0:T(8,128)S(1)} %copy-done, f32[1024,256]{1,0:T(8,128)S(1)} %copy-done.1, bf16[1024,4096]{1,0:T(8,128)(2,1)} %all-gather.9.cloned.1.call-done, bf16[256,4096]{1,0:T(8,128)(2,1)} %all-gather.7.cloned.1.call-done, f32[128,8,2,128]{3,2,1,0:T(2,128)S(1)} %bitcast.23), kind=kOutput, calls=%fused_computation.9 | convolution fusion | flops 2148532224 | bytes 14155776 | tf_op jit(solution)/shard_map/dot_general | solution.py:37
  239.3 0.0 all-gather.11.cloned.1.call-update
  239.4 78.7 %all-gather.11.cloned.1.call-done = bf16[1024,4096]{1,0:T(8,128)(2,1)} async-done(((bf16[1024,256]{1,0:T(8,128)(2,1)}), bf16[1024,4096]{1,0:T(8,128)(2,1)}) %all-gather.11.cloned.1.call-update) | async-done | bytes 8388624 | tf_op jit(solution)/shard_map/all_gather | solution.py:36
  318.0 7.3 %fusion.7 = f32[1024,256]{1,0:T(8,128)} fusion(f32[1024,256]{1,0:T(8,128)S(1)} %copy-done, f32[1024,256]{1,0:T(8,128)S(1)} %copy-done.1, bf16[1024,4096]{1,0:T(8,128)(2,1)} %all-gather.11.cloned.1.call-done, bf16[256,4096]{1,0:T(8,128)(2,1)} %all-gather.7.cloned.1.call-done, f32[128,8,2,128]{3,2,1,0:T(2,128)S(1)} %bitcast.24), kind=kOutput, calls=%fused_computation.10 | convolution fusion | flops 2148270080 | bytes 14680064 | tf_op jit(solution)/shard_map/dot_general | solution.py:37
Async XLA Ops:
  6.5 56.5 %all-gather.7.cloned.1.call-start = ((), (), s32[]{:S(2)}) async-start(), calls=%async_computation.1 | async-start | bytes 2359296 | tf_op jit(solution)/shard_map/all_gather | solution.py:39
  9.2 136.6 %all-gather.5.cloned.1.call-start = ((), (), s32[]{:S(2)}) async-start(), calls=%async_computation | async-start | bytes 8912896 | tf_op jit(solution)/shard_map/all_gather | solution.py:36
  13.8 218.4 %copy-start = (f32[1024,256]{1,0:T(8,128)S(1)}, f32[1024,256]{1,0:T(8,128)}, u32[]{:S(2)}) copy-start(f32[1024,256]{1,0:T(8,128)} %param.7) | copy-start | bytes 3145732
  13.8 218.4 %copy-start.1 = (f32[1024,256]{1,0:T(8,128)S(1)}, f32[1024,256]{1,0:T(8,128)}, u32[]{:S(2)}) copy-start(f32[1024,256]{1,0:T(8,128)} %param.6) | copy-start | bytes 3145732
  13.8 218.3 %all-gather.9.cloned.1.call-start = ((), (), s32[]{:S(2)}) async-start(), calls=%async_computation.2 | async-start | bytes 8912896 | tf_op jit(solution)/shard_map/all_gather | solution.py:36
  153.5 164.5 %all-gather.11.cloned.1.call-start = ((), (), s32[]{:S(2)}) async-start(), calls=%async_computation.3 | async-start | bytes 8912896 | tf_op jit(solution)/shard_map/all_gather | solution.py:36
Sparse Core Ops, SparseCore 0:
  9.3 53.6 all-gather.6
  65.3 80.4 all-gather.4
  153.6 78.5 all-gather.8
  239.5 78.5 all-gather.10
where the time goes:
time: 333 us; the launch traced here: 332 us
  waiting for transfers between devices  289 us (87%)
  matrix products  22.2 us (7%)
  between operations  13.2 us (4%)
  other arithmetic  5.94 us (2%)
    all_gather x3, waiting for transfers between devices, local(): gathered = lax.all_gather(rounded, 'bcast', axis=1, tiled=True)  240 us
    all_gather x1, waiting for transfers between devices, local(): lax.all_gather(screened, 'blk', axis=1, tiled=True)  49.1 us
    dot_general x3, matrix products, local(): lax.dot_general(gathered, lax.all_gather(screened, 'blk', axis=1, tiled=T...  22.2 us
  transfers between devices with their start and end apart: 4, of which 4 were waited for; matrix products, arithmetic and copies ran while one was open for 1% of the time, Pallas kernels for 0%

commit v1 on v0

v1 whole, which is shorter than its diff:
```python
import jax
import jax.numpy as jnp
from jax import lax
from jax.experimental import pallas as pl
from jax.experimental.pallas import tpu as pltpu
from jax.sharding import PartitionSpec as P

TILE = 128
ROW_TILE = 128
ITERS = 3
MESH = pl.DeviceIdType.MESH

ROWS = 1024
COLS = 256
CHUNK = 128
CHUNKS = ROWS // CHUNK
STEPS = ITERS * CHUNKS
HALF = CHUNK // 2
FINAL = 3
FORWARD = 5
RING = 4


def device(x, y, z, core):
    x, y, z, core = x % 4, y % 4, z % 4, core % 2
    return (x * 2 + z % 2, ((z // 2) * 4 + y) * 2 + core)


def kernel(
    sizes_ref,
    ov_ref,
    vv_ref,
    coupling_ref,
    den_ref,
    integrals_ref,
    out_ref,
    weight,
    amp,
    mine,
    table,
    sib_out,
    own,
    sib_in,
    z_out,
    z_in,
    up_send,
    down_send,
    up_recv,
    down_recv,
    fup_send,
    fdown_send,
    fup_recv,
    fdown_recv,
    sib_send,
    sib_recv,
    z_send,
    z_recv,
    t_send,
    t_recv,
):
    blk = lax.axis_index("blk")
    bcast = lax.axis_index("bcast")
    x, zl = blk // 2, blk % 2
    zh, y, core = bcast // 8, (bcast // 2) % 4, bcast % 2
    z = zh * 2 + zl
    up = device(x, y + 1, z, core)
    down = device(x, y + 3, z, core)
    sibling = device(x, y, z, core + 1)
    across = device(x, y, z + 2, core)
    inside = (x // 2) == zh

    barrier = pltpu.get_barrier_semaphore()

    def greet(dev):
        pl.semaphore_signal(barrier, inc=1, device_id=dev, device_id_type=MESH)

    for dev in (up, down, sibling, across):
        greet(dev)
    for i in range(2):
        for dz in range(4):
            for dc in range(2):
                source = device(2 * zh + (x % 2 + i) % 2, y, z + dz, core + dc)
                if i == 0 and dz == 0 and dc == 0:
                    pl.when(jnp.logical_not(inside))(lambda s=source: greet(s))
                else:
                    greet(source)

    for h in range(2):
        for j in range(2):
            for i in range(2):
                keep = vv_ref[bcast * 2 + i, blk * 4 + h * 2 + j].astype(jnp.float32)
                part = integrals_ref[
                    pl.ds(i * TILE, TILE), pl.ds((h * 2 + j) * TILE, TILE)
                ].astype(jnp.float32)
                mine[h, pl.ds(j * TILE, TILE), pl.ds(i * TILE, TILE)] = (
                    jnp.transpose(part * keep).astype(jnp.bfloat16)
                )

    size0 = sizes_ref[bcast * 2]
    size1 = sizes_ref[bcast * 2 + 1]

    def rows_of(k):
        return pl.ds(pl.multiple_of(k * CHUNK, CHUNK), CHUNK)

    def first_amplitudes(k):
        lane = lax.broadcasted_iota(jnp.int32, (CHUNK, COLS), 1)
        ov0 = ov_ref[blk * CHUNKS + k, bcast * 2]
        ov1 = ov_ref[blk * CHUNKS + k, bcast * 2 + 1]
        live0 = jnp.where(lane < size0, ov0, 0)
        live1 = jnp.where(lane - TILE < size1, ov1, 0)
        keep = jnp.where(lane < TILE, live0, live1).astype(jnp.float32)
        w = keep / den_ref[rows_of(k), :]
        weight[rows_of(k), :] = w
        amp[0, y, rows_of(k), :] = (coupling_ref[rows_of(k), :] * w).astype(jnp.bfloat16)

    def part_of(t, owner, k, offset, length):
        start = pl.multiple_of(k * CHUNK + offset, HALF)
        return amp.at[t, owner, pl.ds(start, length), :]

    def remote(ref, target, send, recv):
        return pltpu.make_async_remote_copy(
            src_ref=ref, dst_ref=ref, send_sem=send, recv_sem=recv,
            device_id=target, device_id_type=MESH,
        )

    def send_up(s):
        ref = part_of(s // CHUNKS, y, s % CHUNKS, 0, CHUNK)
        return remote(ref, up, up_send.at[s], up_recv.at[s])

    def send_down(s):
        ref = part_of(s // CHUNKS, y, s % CHUNKS, 0, CHUNK)
        return remote(ref, down, down_send.at[s], down_recv.at[s])

    below, above, far = (y + 3) % RING, (y + 1) % RING, (y + 2) % RING

    def from_below(s):
        ref = part_of(s // CHUNKS, below, s % CHUNKS, 0, CHUNK)
        return remote(ref, up, up_send.at[s], up_recv.at[s])

    def from_above(s):
        ref = part_of(s // CHUNKS, above, s % CHUNKS, 0, CHUNK)
        return remote(ref, down, down_send.at[s], down_recv.at[s])

    def pass_up(s):
        ref = part_of(s // CHUNKS, below, s % CHUNKS, 0, HALF)
        return remote(ref, up, fup_send.at[s], fup_recv.at[s])

    def pass_down(s):
        ref = part_of(s // CHUNKS, above, s % CHUNKS, HALF, HALF)
        return remote(ref, down, fdown_send.at[s], fdown_recv.at[s])

    def far_from_below(s):
        ref = part_of(s // CHUNKS, far, s % CHUNKS, 0, HALF)
        return remote(ref, up, fup_send.at[s], fup_recv.at[s])

    def far_from_above(s):
        ref = part_of(s // CHUNKS, far, s % CHUNKS, HALF, HALF)
        return remote(ref, down, fdown_send.at[s], fdown_recv.at[s])

    def to_sibling(s):
        return pltpu.make_async_remote_copy(
            src_ref=sib_out.at[s % CHUNKS], dst_ref=sib_in.at[s],
            send_sem=sib_send.at[s], recv_sem=sib_recv.at[s],
            device_id=sibling, device_id_type=MESH,
        )

    def to_across(s):
        return pltpu.make_async_remote_copy(
            src_ref=z_out.at[s % CHUNKS], dst_ref=z_in.at[s],
            send_sem=z_send.at[s], recv_sem=z_recv.at[s],
            device_id=across, device_id_type=MESH,
        )

    def start_ring(s):
        send_up(s).start()
        send_down(s).start()

    def forward(s):
        from_below(s).wait_recv()
        pass_up(s).start()
        from_above(s).wait_recv()
        pass_down(s).start()

    def product(s):
        far_from_below(s).wait_recv()
        far_from_above(s).wait_recv()
        t, k = s // CHUNKS, s % CHUNKS
        lhs = jnp.concatenate([amp[t, o, rows_of(k), :] for o in range(RING)], axis=1)
        for h in range(2):
            sib_out[k, h] = jnp.dot(
                lhs, table[h * 2 + (1 - core)], preferred_element_type=jnp.float32
            )
        to_sibling(s).start()
        for h in range(2):
            own[k, h] = jnp.dot(
                lhs, table[h * 2 + core], preferred_element_type=jnp.float32
            )

    def reduce_core(s):
        k = s % CHUNKS
        to_sibling(s).wait()
        z_out[k] = (own[k, 1 - zh] + sib_in[s, 1 - zh]).astype(jnp.bfloat16)
        to_across(s).start()

    def finish(s):
        t, k = s // CHUNKS, s % CHUNKS
        to_across(s).wait()
        ladder = own[k, zh] + sib_in[s, zh] + z_in[s].astype(jnp.float32)
        value = (coupling_ref[rows_of(k), :] + ladder) * weight[rows_of(k), :]

        @pl.when(t < ITERS - 1)
        def _():
            amp[t + 1, y, rows_of(k), :] = value.astype(jnp.bfloat16)
            start_ring(s + CHUNKS)

        @pl.when(t == ITERS - 1)
        def _():
            out_ref[rows_of(k), :] = value

        send_up(s).wait_send()
        send_down(s).wait_send()
        pass_up(s).wait_send()
        pass_down(s).wait_send()

    first_amplitudes(0)
    pl.semaphore_wait(barrier, 20 - inside.astype(jnp.int32))
    start_ring(0)

    block = zh * 2 + core
    place = (x % 2) * 2 + zl
    landing = pl.ds(pl.multiple_of(place * COLS, COLS), COLS)
    sends = []
    for dx in range(4):
        for dl in range(2):
            for dc in range(2):
                n = dx * 4 + dl * 2 + dc
                target = device(x + dx, y, 2 * (x // 2) + (zl + dl) % 2, core + dc)
                copy = pltpu.make_async_remote_copy(
                    src_ref=mine.at[(core + dc) % 2],
                    dst_ref=table.at[block, landing, :],
                    send_sem=t_send.at[n],
                    recv_sem=t_recv.at[block * 4 + place],
                    device_id=target,
                    device_id_type=MESH,
                )
                sends.append(copy)
    local = pltpu.make_async_copy(
        mine.at[core], table.at[block, landing, :], t_recv.at[block * 4 + place]
    )
    for n, copy in enumerate(sends):
        if n == 0:
            pl.when(inside)(local.start)
            pl.when(jnp.logical_not(inside))(copy.start)
        else:
            copy.start()

    @pl.loop(1, CHUNKS)
    def _(k):
        first_amplitudes(k)
        start_ring(k)

    @pl.loop(0, CHUNKS)
    def _(k):
        forward(k)

    @pl.loop(0, 16)
    def _(n):
        ref = table.at[n // 4, pl.ds(pl.multiple_of((n % 4) * COLS, COLS), COLS), :]
        pltpu.make_async_remote_copy(
            src_ref=ref, dst_ref=ref, send_sem=t_send.at[n], recv_sem=t_recv.at[n],
            device_id=sibling, device_id_type=MESH,
        ).wait_recv()

    @pl.loop(0, STEPS + FINAL)
    def _(tick):
        @pl.when(jnp.logical_and(tick >= FINAL, tick < STEPS + FINAL))
        def _():
            finish(tick - FINAL)

        @pl.when(jnp.logical_and(tick >= FORWARD, tick < STEPS - CHUNKS + FORWARD))
        def _():
            forward(tick - FORWARD + CHUNKS)

        @pl.when(jnp.logical_and(tick >= 1, tick < STEPS + 1))
        def _():
            reduce_core(tick - 1)

        @pl.when(tick < STEPS)
        def _():
            product(tick)

    pl.when(jnp.logical_not(inside))(sends[0].wait_send)
    for copy in sends[1:]:
        copy.wait_send()


def local(coupling, denominators, integrals, tile_sizes, screen_ov, screen_vv):
    dma = pltpu.SemaphoreType.DMA
    smem = pl.BlockSpec(memory_space=pltpu.SMEM)
    vmem = pl.BlockSpec(memory_space=pltpu.VMEM)
    return pl.pallas_call(
        kernel,
        out_shape=jax.ShapeDtypeStruct((ROWS, COLS), jnp.float32),
        in_specs=[smem] * 3 + [vmem] * 3,
        out_specs=vmem,
        scratch_shapes=[
            pltpu.VMEM((ROWS, COLS), jnp.float32),
            pltpu.VMEM((ITERS, RING, ROWS, COLS), jnp.bfloat16),
            pltpu.VMEM((2, COLS, COLS), jnp.bfloat16),
            pltpu.VMEM((4, RING * COLS, COLS), jnp.bfloat16),
            pltpu.VMEM((CHUNKS, 2, CHUNK, COLS), jnp.float32),
            pltpu.VMEM((CHUNKS, 2, CHUNK, COLS), jnp.float32),
            pltpu.VMEM((STEPS, 2, CHUNK, COLS), jnp.float32),
            pltpu.VMEM((CHUNKS, CHUNK, COLS), jnp.bfloat16),
            pltpu.VMEM((STEPS, CHUNK, COLS), jnp.bfloat16),
        ]
        + [dma((STEPS,))] * 12
        + [dma((16,))] * 2,
        compiler_params=pltpu.CompilerParams(
            collective_id=0, has_side_effects=True, vmem_limit_bytes=48 * 1024 * 1024
        ),
        cost_estimate=pl.CostEstimate(
            flops=3 * 2 * ROWS * 1024 * 1024,
            bytes_accessed=4 * 1024 * 1024,
            transcendentals=0,
        ),
    )(tile_sizes, screen_ov, screen_vv, coupling, denominators, integrals)


def solution(mesh):
    in_specs = (P("blk", "bcast"), P("blk", "bcast"), P("bcast", "blk"), P(), P(), P())
    out_specs = P("blk", "bcast")
    return jax.shard_map(local, mesh=mesh, in_specs=in_specs, out_specs=out_specs, check_vma=False)
```

time: 333 us -> 99.6 us (0.30)
  waiting for transfers between devices: 289 us -> 0 us
  Pallas kernels: 0 us -> 93.8 us
  matrix products: 22.2 us -> 0 us
  between operations: 13.2 us -> 0.03 us
  other arithmetic: 5.94 us -> 0 us
  local copies, waits for them, and re-layouts: 1.24 us -> 5.2 us
    all_gather x4 -> x0, waiting for transfers between devices: 289 us -> none  [the longest x3 240 us: local(): gathered = lax.all_gather(rounded, 'bcast', axis=1, tiled=True)]
    pallas_call x0 -> x1, Pallas kernels: none -> 93.8 us  [local(): pl.pallas_call(kernel, out_shape=jax.ShapeDtypeStruct((ROWS, COLS), jnp.f...]
    dot_general x3 -> x0, matrix products: 22.2 us -> none  [local(): lax.dot_general(gathered, lax.all_gather(screened, 'blk', axis=1, tiled=T...]
    unnamed x4 -> x12, local copies, waits for them, and re-layouts: 0.01 us -> 5.2 us
    convert_element_type x4 -> x0, other arithmetic: 4.15 us -> none  [the longest x1 2.56 us: local(): rounded = amplitudes.astype(jnp.bfloat16)]
  transfers between devices with their start and end apart: 4 -> 0, of which waited for: 4 -> 0; matrix products, arithmetic and copies ran while one was open for 1% -> 0% of each run, Pallas kernels for 0% -> 0%
where the time goes in v1:
time: 99.6 us; the launch traced here: 99 us
  Pallas kernels  93.8 us (94%)
  local copies, waits for them, and re-layouts  5.2 us (5%)
    pallas_call x1, Pallas kernels, local(): pl.pallas_call(kernel, out_shape=jax.ShapeDtypeStruct((ROWS, COLS), jnp.f...  93.8 us
    unnamed x12, local copies, waits for them, and re-layouts  5.2 us

profile of v1, /device:TPU:0, one launch (start us, length us, event | category | flops | bytes accessed | tf_op | source)
XLA Modules:
  0.0 99.0 jit_solution(5318943080670555272)
XLA Ops:
  0.0 0.0 copy-start.3
  0.0 0.0 copy-start.4
  0.0 0.8 copy.7.ov_ref
  0.8 0.0 copy-done.3
  0.8 0.0 copy-done.4
  0.8 0.0 copy-start
  0.9 1.2 %copy-done = f32[1024,256]{1,0:T(8,128)S(1)} copy-done((f32[1024,256]{1,0:T(8,128)S(1)}, f32[1024,256]{1,0:T(8,128)}, u32[]{:S(2)}) %copy-start) | copy-done | bytes 1048600
  2.1 0.0 copy-start.1
  2.1 1.2 %copy-done.1 = f32[1024,256]{1,0:T(8,128)S(1)} copy-done((f32[1024,256]{1,0:T(8,128)S(1)}, f32[1024,256]{1,0:T(8,128)}, u32[]{:S(2)}) %copy-start.1) | copy-done | bytes 1048600
  3.3 0.0 copy-start.2
  3.3 0.9 copy-done.2
  4.2 93.8 %shard_map.64 = f32[1024,256]{1,0:T(8,128)S(1)} custom-call(s32[32]{0:T(128)S(1)} %copy-done.4, s32[64,32]{1,0:T(8,128)S(1)} %copy.7.ov_ref, s32[32,32]{1,0:T(8,128)S(1)} %copy-done.3, f32[1024,256]{1,0:T(8,128)S(1)} %copy-done, f32[1024,256]{1,0:T(8,128)S(1)} %copy-done.1, bf16[256,512]{1,0:T(8,128)(2,1)S(1)} %copy-done.2), custom_call_target="tpu_custom_call" | custom-call | flops 6442450944 | bytes 4194304 | tf_op jit(solution)/shard_map/pallas_call | solution.py:301
  98.1 1.0 copy.9
Async XLA Ops:
  0.0 0.8 copy-start.3
  0.0 0.8 copy-start.4
  0.8 1.2 %copy-start = (f32[1024,256]{1,0:T(8,128)S(1)}, f32[1024,256]{1,0:T(8,128)}, u32[]{:S(2)}) copy-start(f32[1024,256]{1,0:T(8,128)} %coupling_ref.1) | copy-start | bytes 3145732
  2.1 1.2 %copy-start.1 = (f32[1024,256]{1,0:T(8,128)S(1)}, f32[1024,256]{1,0:T(8,128)}, u32[]{:S(2)}) copy-start(f32[1024,256]{1,0:T(8,128)} %den_ref.1) | copy-start | bytes 3145732
  3.3 0.9 copy-start.2

commit v2 on v1

--- a/solution.py
+++ b/solution.py
@@ -36,7 +36,9 @@
     out_ref,
     weight,
     amp,
-    mine,
+    swap,
+    unit,
+    ring,
     table,
     sib_out,
     own,
@@ -55,7 +57,12 @@
     sib_recv,
     z_send,
     z_recv,
-    t_send,
+    swap_send,
+    swap_recv,
+    ring_send,
+    ring_recv,
+    o_send,
+    s_send,
     t_recv,
 ):
     blk = lax.axis_index("blk")
@@ -67,34 +74,33 @@
     down = device(x, y + 3, z, core)
     sibling = device(x, y, z, core + 1)
     across = device(x, y, z + 2, core)
+    x_pair, x_out = x + 1 - 2 * (x % 2), x - 1 + 2 * (x % 2)
+    z_mate, z_next = z + 1 - 2 * zl, z - 1 + 2 * zl
+    pair_x = device(x_pair, y, z, core)
+    out_x = device(x_out + 4, y, z, core)
+    pair_z = device(x, y, z_mate, core)
+    out_z = device(x, y, z_next + 4, core)
+    right = device(x + 1, y, z, core)
+    left = device(x + 3, y, z, core)
     inside = (x // 2) == zh
+    outside = jnp.logical_not(inside)
 
     barrier = pltpu.get_barrier_semaphore()
-
-    def greet(dev):
+    for dev in (up, down, sibling, across, pair_x, out_x, pair_z, out_z):
         pl.semaphore_signal(barrier, inc=1, device_id=dev, device_id_type=MESH)
 
-    for dev in (up, down, sibling, across):
-        greet(dev)
-    for i in range(2):
-        for dz in range(4):
-            for dc in range(2):
-                source = device(2 * zh + (x % 2 + i) % 2, y, z + dz, core + dc)
-                if i == 0 and dz == 0 and dc == 0:
-                    pl.when(jnp.logical_not(inside))(lambda s=source: greet(s))
-                else:
-                    greet(source)
-
-    for h in range(2):
+    def screened(h, ref):
         for j in range(2):
             for i in range(2):
                 keep = vv_ref[bcast * 2 + i, blk * 4 + h * 2 + j].astype(jnp.float32)
-                part = integrals_ref[
-                    pl.ds(i * TILE, TILE), pl.ds((h * 2 + j) * TILE, TILE)
-                ].astype(jnp.float32)
-                mine[h, pl.ds(j * TILE, TILE), pl.ds(i * TILE, TILE)] = (
-                    jnp.transpose(part * keep).astype(jnp.bfloat16)
-                )
+                at = pl.ds(pl.multiple_of((h * 2 + j) * TILE, TILE), TILE)
+                part = integrals_ref[pl.ds(i * TILE, TILE), at].astype(jnp.float32)
+                ref[pl.ds(j * TILE, TILE), pl.ds(i * TILE, TILE)] = jnp.transpose(
+                    part * keep
+                ).astype(jnp.bfloat16)
+
+    screened(1 - core, swap)
+    screened(core, ring.at[x])
 
     size0 = sizes_ref[bcast * 2]
     size1 = sizes_ref[bcast * 2 + 1]
@@ -222,54 +228,158 @@
         pass_up(s).wait_send()
         pass_down(s).wait_send()
 
-    first_amplitudes(0)
-    pl.semaphore_wait(barrier, 20 - inside.astype(jnp.int32))
-    start_ring(0)
-
-    block = zh * 2 + core
-    place = (x % 2) * 2 + zl
-    landing = pl.ds(pl.multiple_of(place * COLS, COLS), COLS)
-    sends = []
-    for dx in range(4):
-        for dl in range(2):
-            for dc in range(2):
-                n = dx * 4 + dl * 2 + dc
-                target = device(x + dx, y, 2 * (x // 2) + (zl + dl) % 2, core + dc)
-                copy = pltpu.make_async_remote_copy(
-                    src_ref=mine.at[(core + dc) % 2],
-                    dst_ref=table.at[block, landing, :],
-                    send_sem=t_send.at[n],
-                    recv_sem=t_recv.at[block * 4 + place],
-                    device_id=target,
-                    device_id_type=MESH,
-                )
-                sends.append(copy)
-    local = pltpu.make_async_copy(
-        mine.at[core], table.at[block, landing, :], t_recv.at[block * 4 + place]
+    def slot_of(first_core, zh_of, parity, zl_of):
+        return (zh_of * 2 + first_core) * 4 + parity * 2 + zl_of
+
+    def at_slot(slot):
+        start = pl.multiple_of((slot % 4) * COLS, COLS)
+        return table.at[slot // 4, pl.ds(start, COLS), :]
+
+    def unit_copy(src, slot, send, target):
+        return pltpu.make_async_remote_copy(
+            src_ref=src, dst_ref=at_slot(slot), send_sem=send, recv_sem=t_recv.at[slot],
+            device_id=target, device_id_type=MESH,
+        )
+
+    def arrived(slot):
+        unit_copy(at_slot(slot), slot, swap_send, sibling).wait_recv()
+
+    to_swap = pltpu.make_async_remote_copy(
+        src_ref=swap, dst_ref=unit, send_sem=swap_send, recv_sem=swap_recv,
+        device_id=sibling, device_id_type=MESH,
     )
-    for n, copy in enumerate(sends):
-        if n == 0:
-            pl.when(inside)(local.start)
-            pl.when(jnp.logical_not(inside))(copy.start)
-        else:
-            copy.start()
-
-    @pl.loop(1, CHUNKS)
-    def _(k):
+    parity = x % 2
+
+    def ring_part(owner, half):
+        owner = (owner + 4) % 4
+        if half is None:
+            return ring.at[owner]
+        return ring.at[owner, pl.ds(half * TILE, TILE), :]
+
+    def ring_copy(owner, half, n, target):
+        ref = ring_part(owner, half)
+        return remote(ref, target, ring_send.at[n], ring_recv.at[n])
+
+    def o_slot(owner):
+        return slot_of(core, zh, owner % 2, zl)
+
+    def over_z(n):
+        owner = (x + (0, 3, 1, 2)[n]) % 4
+        target = tuple(
+            jnp.where(owner // 2 == zh, a, b) for a, b in zip(pair_z, out_z)
+        )
+        return unit_copy(ring.at[owner], o_slot(owner), o_send.at[n], target)
+
+    def o_pass(n):
+        slot = slot_of(core, 1 - zh, n, 1 - zl)
+        return unit_copy(at_slot(slot), slot, o_send.at[4 + n], pair_z)
+
+    s_slots = [
+        lambda par, a=a, b=b: slot_of(1 - core, a, par, b)
+        for a, b in ((zh, zl), (zh, 1 - zl), (1 - zh, 1 - zl), (1 - zh, zl))
+    ]
+    first_target = tuple(jnp.where(inside, a, b) for a, b in zip(pair_z, out_z))
+    s_first = unit_copy(unit, s_slots[0](parity), s_send.at[0], first_target)
+    s_pass = unit_copy(
+        at_slot(s_slots[2](parity)), s_slots[2](parity), s_send.at[1], pair_z
+    )
+
+    def s_inside(n, k):
+        slot = s_slots[n](parity)
+        src = unit if n == 0 else at_slot(slot)
+        return unit_copy(src, slot, s_send.at[2 + 2 * n + k], (pair_x, out_x)[k])
+
+    def s_outside(n):
+        slot = s_slots[n](1 - parity)
+        return unit_copy(at_slot(slot), slot, s_send.at[2 + 2 * n], pair_x)
+
+    def s_start(n):
+        s_inside(n, 1).start()
+        s_inside(n, 0).start()
+
+    def s_relay(n):
+        arrived(s_slots[n](1 - parity))
+        s_outside(n).start()
+
+    def new_chunk(k):
         first_amplitudes(k)
         start_ring(k)
 
-    @pl.loop(0, CHUNKS)
+    first_amplitudes(0)
+    pl.semaphore_wait(barrier, 8)
+    to_swap.start()
+    ring_copy(x, None, 0, right).start()
+    ring_copy(x, None, 1, left).start()
+    start_ring(0)
+    over_z(0).start()
+    new_chunk(1)
+
+    to_swap.wait_recv()
+    s_first.start()
+
+    @pl.when(inside)
+    def _():
+        s_start(0)
+        table[(zh * 2 + 1 - core), pl.ds(pl.multiple_of((parity * 2 + zl) * COLS, COLS), COLS), :] = unit[...]
+
+    @pl.loop(2, 5)
     def _(k):
-        forward(k)
-
-    @pl.loop(0, 16)
-    def _(n):
-        ref = table.at[n // 4, pl.ds(pl.multiple_of((n % 4) * COLS, COLS), COLS), :]
-        pltpu.make_async_remote_copy(
-            src_ref=ref, dst_ref=ref, send_sem=t_send.at[n], recv_sem=t_recv.at[n],
-            device_id=sibling, device_id_type=MESH,
-        ).wait_recv()
+        new_chunk(k)
+
+    ring_copy(x + 3, None, 0, right).wait_recv()
+    ring_copy(x + 3, 0, 2, right).start()
+    over_z(1).start()
+    ring_copy(x + 1, None, 1, left).wait_recv()
+    ring_copy(x + 1, 1, 3, left).start()
+    over_z(2).start()
+
+    @pl.loop(5, CHUNKS)
+    def _(k):
+        new_chunk(k)
+
+    forward(0)
+
+    @pl.when(inside)
+    def _():
+        arrived(s_slots[1](parity))
+        s_start(1)
+        arrived(s_slots[2](parity))
+        s_pass.start()
+        s_start(2)
+
+    @pl.when(outside)
+    def _():
+        s_relay(0)
+
+    ring_copy(x + 2, 0, 2, right).wait_recv()
+    ring_copy(x + 2, 1, 3, left).wait_recv()
+    over_z(3).start()
+    for p in range(2):
+        owner = 2 * zh + p
+        table[zh * 2 + core, pl.ds(pl.multiple_of((p * 2 + zl) * COLS, COLS), COLS), :] = ring[owner]
+    forward(1)
+    forward(2)
+    pl.when(outside)(lambda: s_relay(1))
+    forward(3)
+
+    @pl.when(inside)
+    def _():
+        arrived(s_slots[3](parity))
+        s_start(3)
+
+    pl.when(outside)(lambda: s_relay(2))
+    for n in range(2):
+        arrived(slot_of(core, 1 - zh, n, 1 - zl))
+        o_pass(n).start()
+        forward(4 + n)
+    pl.when(outside)(lambda: s_relay(3))
+    forward(6)
+    forward(7)
+    for n in range(2):
+        arrived(slot_of(core, zh, n, 1 - zl))
+        arrived(slot_of(core, 1 - zh, n, zl))
+    for n in range(4):
+        arrived(s_slots[n](jnp.where(inside, 1 - parity, parity)))
 
     @pl.loop(0, STEPS + FINAL)
     def _(tick):
@@ -289,9 +399,26 @@
         def _():
             product(tick)
 
-    pl.when(jnp.logical_not(inside))(sends[0].wait_send)
-    for copy in sends[1:]:
-        copy.wait_send()
+    to_swap.wait_send()
+    for n, (owner, half) in enumerate(((x, None), (x, None), (x + 3, 0), (x + 1, 1))):
+        ring_copy(owner, half, n, right).wait_send()
+    for n in range(4):
+        over_z(n).wait_send()
+    o_pass(0).wait_send()
+    o_pass(1).wait_send()
+    s_first.wait_send()
+
+    @pl.when(inside)
+    def _():
+        s_pass.wait_send()
+        for n in range(4):
+            for k in range(2):
+                s_inside(n, k).wait_send()
+
+    @pl.when(outside)
+    def _():
+        for n in range(4):
+            s_outside(n).wait_send()
 
 
 def local(coupling, denominators, integrals, tile_sizes, screen_ov, screen_vv):
@@ -306,7 +433,9 @@
         scratch_shapes=[
             pltpu.VMEM((ROWS, COLS), jnp.float32),
             pltpu.VMEM((ITERS, RING, ROWS, COLS), jnp.bfloat16),
-            pltpu.VMEM((2, COLS, COLS), jnp.bfloat16),
+            pltpu.VMEM((COLS, COLS), jnp.bfloat16),
+            pltpu.VMEM((COLS, COLS), jnp.bfloat16),
+            pltpu.VMEM((4, COLS, COLS), jnp.bfloat16),
             pltpu.VMEM((4, RING * COLS, COLS), jnp.bfloat16),
             pltpu.VMEM((CHUNKS, 2, CHUNK, COLS), jnp.float32),
             pltpu.VMEM((CHUNKS, 2, CHUNK, COLS), jnp.float32),
@@ -315,7 +444,7 @@
             pltpu.VMEM((STEPS, CHUNK, COLS), jnp.bfloat16),
         ]
         + [dma((STEPS,))] * 12
-        + [dma((16,))] * 2,
+        + [dma, dma, dma((4,)), dma((4,)), dma((6,)), dma((10,)), dma((16,))],
         compiler_params=pltpu.CompilerParams(
             collective_id=0, has_side_effects=True, vmem_limit_bytes=48 * 1024 * 1024
         ),

time: 99.6 us -> 92.2 us (0.926)
  Pallas kernels: 93.8 us -> 86.7 us
    pallas_call x1, Pallas kernels: 93.8 us -> 86.7 us  [local(): pl.pallas_call(kernel, out_shape=jax.ShapeDtypeStruct((ROWS, COLS), jnp.f...]
where the time goes in v2:
time: 92.2 us; the launch traced here: 91.9 us
  Pallas kernels  86.7 us (94%)
  local copies, waits for them, and re-layouts  5.2 us (6%)
    pallas_call x1, Pallas kernels, local(): pl.pallas_call(kernel, out_shape=jax.ShapeDtypeStruct((ROWS, COLS), jnp.f...  86.7 us
    unnamed x12, local copies, waits for them, and re-layouts  5.2 us

profile of v2, /device:TPU:0, one launch (start us, length us, event | category | flops | bytes accessed | tf_op | source)
XLA Modules:
  0.0 91.9 jit_solution(16855420225739623455)
XLA Ops:
  0.0 0.0 copy-start.3
  0.0 0.0 copy-start.4
  0.0 0.8 copy.7.ov_ref
  0.8 0.0 copy-done.3
  0.8 0.0 copy-done.4
  0.8 0.0 copy-start
  0.9 1.2 %copy-done = f32[1024,256]{1,0:T(8,128)S(1)} copy-done((f32[1024,256]{1,0:T(8,128)S(1)}, f32[1024,256]{1,0:T(8,128)}, u32[]{:S(2)}) %copy-start) | copy-done | bytes 1048600
  2.1 0.0 copy-start.1
  2.1 1.2 %copy-done.1 = f32[1024,256]{1,0:T(8,128)S(1)} copy-done((f32[1024,256]{1,0:T(8,128)S(1)}, f32[1024,256]{1,0:T(8,128)}, u32[]{:S(2)}) %copy-start.1) | copy-done | bytes 1048600
  3.3 0.0 copy-start.2
  3.3 0.9 %copy-done.2 = bf16[256,512]{1,0:T(8,128)(2,1)S(1)} copy-done((bf16[256,512]{1,0:T(8,128)(2,1)S(1)}, bf16[256,512]{1,0:T(8,128)(2,1)}, u32[]{:S(2)}) %copy-start.2) | copy-done | bytes 262168
  4.2 86.7 %shard_map.64 = f32[1024,256]{1,0:T(8,128)S(1)} custom-call(s32[32]{0:T(128)S(1)} %copy-done.4, s32[64,32]{1,0:T(8,128)S(1)} %copy.7.ov_ref, s32[32,32]{1,0:T(8,128)S(1)} %copy-done.3, f32[1024,256]{1,0:T(8,128)S(1)} %copy-done, f32[1024,256]{1,0:T(8,128)S(1)} %copy-done.1, bf16[256,512]{1,0:T(8,128)(2,1)S(1)} %copy-done.2), custom_call_target="tpu_custom_call" | custom-call | flops 6442450944 | bytes 4194304 | tf_op jit(solution)/shard_map/pallas_call | solution.py:428
  90.9 1.0 %copy.9 = f32[1024,256]{1,0:T(8,128)} copy(f32[1024,256]{1,0:T(8,128)S(1)} %shard_map.64) | data formatting | bytes 2097152
Async XLA Ops:
  0.0 0.8 copy-start.3
  0.0 0.8 copy-start.4
  0.8 1.2 %copy-start = (f32[1024,256]{1,0:T(8,128)S(1)}, f32[1024,256]{1,0:T(8,128)}, u32[]{:S(2)}) copy-start(f32[1024,256]{1,0:T(8,128)} %coupling_ref.1) | copy-start | bytes 3145732
  2.1 1.2 %copy-start.1 = (f32[1024,256]{1,0:T(8,128)S(1)}, f32[1024,256]{1,0:T(8,128)}, u32[]{:S(2)}) copy-start(f32[1024,256]{1,0:T(8,128)} %den_ref.1) | copy-start | bytes 3145732
  3.3 0.9 %copy-start.2 = (bf16[256,512]{1,0:T(8,128)(2,1)S(1)}, bf16[256,512]{1,0:T(8,128)(2,1)}, u32[]{:S(2)}) copy-start(bf16[256,512]{1,0:T(8,128)(2,1)} %integrals_ref.1) | copy-start | bytes 786436

commit v3 on v2

--- a/solution.py
+++ b/solution.py
@@ -14,10 +14,11 @@
 COLS = 256
 CHUNK = 128
 CHUNKS = ROWS // CHUNK
+SPLIT = ROW_TILE // CHUNK
 STEPS = ITERS * CHUNKS
 HALF = CHUNK // 2
-FINAL = 3
-FORWARD = 5
+FINAL = 4
+FORWARD = 6
 RING = 4
 
 
@@ -27,13 +28,20 @@
 
 
 def kernel(
+    sizes_hbm,
+    ov_hbm,
+    vv_hbm,
+    coupling_hbm,
+    den_hbm,
+    integrals_hbm,
+    out_ref,
     sizes_ref,
     ov_ref,
     vv_ref,
     coupling_ref,
     den_ref,
     integrals_ref,
-    out_ref,
+    loaded,
     weight,
     amp,
     swap,
@@ -85,6 +93,22 @@
     inside = (x // 2) == zh
     outside = jnp.logical_not(inside)
 
+    loads = [
+        pltpu.make_async_copy(src, dst, loaded.at[n])
+        for n, (src, dst) in enumerate(
+            (
+                (vv_hbm, vv_ref),
+                (integrals_hbm, integrals_ref),
+                (sizes_hbm, sizes_ref),
+                (ov_hbm, ov_ref),
+                (coupling_hbm, coupling_ref),
+                (den_hbm, den_ref),
+            )
+        )
+    ]
+    for load in loads:
+        load.start()
+
     barrier = pltpu.get_barrier_semaphore()
     for dev in (up, down, sibling, across, pair_x, out_x, pair_z, out_z):
         pl.semaphore_signal(barrier, inc=1, device_id=dev, device_id_type=MESH)
@@ -99,19 +123,19 @@
                     part * keep
                 ).astype(jnp.bfloat16)
 
+    loads[0].wait()
+    loads[1].wait()
     screened(1 - core, swap)
     screened(core, ring.at[x])
 
-    size0 = sizes_ref[bcast * 2]
-    size1 = sizes_ref[bcast * 2 + 1]
-
     def rows_of(k):
         return pl.ds(pl.multiple_of(k * CHUNK, CHUNK), CHUNK)
 
     def first_amplitudes(k):
         lane = lax.broadcasted_iota(jnp.int32, (CHUNK, COLS), 1)
-        ov0 = ov_ref[blk * CHUNKS + k, bcast * 2]
-        ov1 = ov_ref[blk * CHUNKS + k, bcast * 2 + 1]
+        size0, size1 = sizes_ref[bcast * 2], sizes_ref[bcast * 2 + 1]
+        ov0 = ov_ref[bcast * 2, blk * 8 + k // SPLIT]
+        ov1 = ov_ref[bcast * 2 + 1, blk * 8 + k // SPLIT]
         live0 = jnp.where(lane < size0, ov0, 0)
         live1 = jnp.where(lane - TILE < size1, ov1, 0)
         keep = jnp.where(lane < TILE, live0, live1).astype(jnp.float32)
@@ -301,18 +325,23 @@
         arrived(s_slots[n](1 - parity))
         s_outside(n).start()
 
+    def forwards(eighth):
+        @pl.loop(eighth * (CHUNKS // 8), (eighth + 1) * (CHUNKS // 8))
+        def _(k):
+            forward(k)
+
     def new_chunk(k):
         first_amplitudes(k)
         start_ring(k)
 
-    first_amplitudes(0)
     pl.semaphore_wait(barrier, 8)
     to_swap.start()
     ring_copy(x, None, 0, right).start()
     ring_copy(x, None, 1, left).start()
-    start_ring(0)
     over_z(0).start()
-    new_chunk(1)
+    for load in loads[2:]:
+        load.wait()
+    new_chunk(0)
 
     to_swap.wait_recv()
     s_first.start()
@@ -322,7 +351,7 @@
         s_start(0)
         table[(zh * 2 + 1 - core), pl.ds(pl.multiple_of((parity * 2 + zl) * COLS, COLS), COLS), :] = unit[...]
 
-    @pl.loop(2, 5)
+    @pl.loop(1, CHUNKS // 2)
     def _(k):
         new_chunk(k)
 
@@ -333,11 +362,11 @@
     ring_copy(x + 1, 1, 3, left).start()
     over_z(2).start()
 
-    @pl.loop(5, CHUNKS)
+    @pl.loop(CHUNKS // 2, CHUNKS)
     def _(k):
         new_chunk(k)
 
-    forward(0)
+    forwards(0)
 
     @pl.when(inside)
     def _():
@@ -357,10 +386,10 @@
     for p in range(2):
         owner = 2 * zh + p
         table[zh * 2 + core, pl.ds(pl.multiple_of((p * 2 + zl) * COLS, COLS), COLS), :] = ring[owner]
-    forward(1)
-    forward(2)
+    forwards(1)
+    forwards(2)
     pl.when(outside)(lambda: s_relay(1))
-    forward(3)
+    forwards(3)
 
     @pl.when(inside)
     def _():
@@ -371,10 +400,10 @@
     for n in range(2):
         arrived(slot_of(core, 1 - zh, n, 1 - zl))
         o_pass(n).start()
-        forward(4 + n)
+        forwards(4 + n)
     pl.when(outside)(lambda: s_relay(3))
-    forward(6)
-    forward(7)
+    forwards(6)
+    forwards(7)
     for n in range(2):
         arrived(slot_of(core, zh, n, 1 - zl))
         arrived(slot_of(core, 1 - zh, n, zl))
@@ -423,14 +452,21 @@
 
 def local(coupling, denominators, integrals, tile_sizes, screen_ov, screen_vv):
     dma = pltpu.SemaphoreType.DMA
-    smem = pl.BlockSpec(memory_space=pltpu.SMEM)
+    anywhere = pl.BlockSpec(memory_space=pl.ANY)
     vmem = pl.BlockSpec(memory_space=pltpu.VMEM)
     return pl.pallas_call(
         kernel,
         out_shape=jax.ShapeDtypeStruct((ROWS, COLS), jnp.float32),
-        in_specs=[smem] * 3 + [vmem] * 3,
+        in_specs=[anywhere] * 6,
         out_specs=vmem,
         scratch_shapes=[
+            pltpu.SMEM((32,), jnp.int32),
+            pltpu.SMEM((32, 64), jnp.int32),
+            pltpu.SMEM((32, 32), jnp.int32),
+            pltpu.VMEM((ROWS, COLS), jnp.float32),
+            pltpu.VMEM((ROWS, COLS), jnp.float32),
+            pltpu.VMEM((COLS, 2 * COLS), jnp.bfloat16),
+            dma((6,)),
             pltpu.VMEM((ROWS, COLS), jnp.float32),
             pltpu.VMEM((ITERS, RING, ROWS, COLS), jnp.bfloat16),
             pltpu.VMEM((COLS, COLS), jnp.bfloat16),
@@ -446,14 +482,14 @@
         + [dma((STEPS,))] * 12
         + [dma, dma, dma((4,)), dma((4,)), dma((6,)), dma((10,)), dma((16,))],
         compiler_params=pltpu.CompilerParams(
-            collective_id=0, has_side_effects=True, vmem_limit_bytes=48 * 1024 * 1024
+            collective_id=0, has_side_effects=True, vmem_limit_bytes=56 * 1024 * 1024
         ),
         cost_estimate=pl.CostEstimate(
             flops=3 * 2 * ROWS * 1024 * 1024,
             bytes_accessed=4 * 1024 * 1024,
             transcendentals=0,
         ),
-    )(tile_sizes, screen_ov, screen_vv, coupling, denominators, integrals)
+    )(tile_sizes, screen_ov.T, screen_vv, coupling, denominators, integrals)
 
 
 def solution(mesh):

time: 92.2 us -> 85.6 us (0.928)
  Pallas kernels: 86.7 us -> 82.5 us
  local copies, waits for them, and re-layouts: 5.2 us -> 2.26 us
    pallas_call x1, Pallas kernels: 86.7 us -> 82.5 us  [local(): pl.pallas_call(kernel, out_shape=jax.ShapeDtypeStruct((ROWS, COLS), jnp.f...]
    unnamed x12 -> x1, local copies, waits for them, and re-layouts: 5.2 us -> 2.26 us
where the time goes in v3:
time: 85.6 us; the launch traced here: 84.8 us
  Pallas kernels  82.5 us (96%)
  local copies, waits for them, and re-layouts  2.26 us (3%)
    pallas_call x1, Pallas kernels, local(): pl.pallas_call(kernel, out_shape=jax.ShapeDtypeStruct((ROWS, COLS), jnp.f...  82.5 us
    unnamed x1, local copies, waits for them, and re-layouts  2.26 us

profile of v3, /device:TPU:0, one launch (start us, length us, event | category | flops | bytes accessed | tf_op | source)
XLA Modules:
  0.0 84.8 jit_solution(4213173373517592579)
XLA Ops:
  0.0 82.5 %shard_map.64 = f32[1024,256]{1,0:T(8,128)} custom-call(s32[32]{0:T(128)} %sizes_hbm.1, s32[32,64]{1,0:T(8,128)} %bitcast.1, s32[32,32]{1,0:T(8,128)} %vv_hbm.1, f32[1024,256]{1,0:T(8,128)} %coupling_hbm.1, f32[1024,256]{1,0:T(8,128)} %den_hbm.1, bf16[256,512]{1,0:T(8,128)(2,1)} %integrals_hbm.1), custom_call_target="tpu_custom_call" | custom-call | flops 6442450944 | bytes 4194304 | tf_op jit(solution)/shard_map/pallas_call | solution.py:457
  82.5 2.3 %copy.8 = f32[1024,256]{1,0:T(8,128)} copy(f32[1024,256]{1,0:T(8,128)} %shard_map.64) | data formatting | bytes 2097152

commit v4 on v3

--- a/solution.py
+++ b/solution.py
@@ -18,6 +18,7 @@
 STEPS = ITERS * CHUNKS
 HALF = CHUNK // 2
 FINAL = 4
+SECOND = 2
 FORWARD = 6
 RING = 4
 
@@ -34,7 +35,7 @@
     coupling_hbm,
     den_hbm,
     integrals_hbm,
-    out_ref,
+    out_hbm,
     sizes_ref,
     ov_ref,
     vv_ref,
@@ -42,6 +43,8 @@
     den_ref,
     integrals_ref,
     loaded,
+    result,
+    stored,
     weight,
     amp,
     swap,
@@ -106,12 +109,11 @@
             )
         )
     ]
-    for load in loads:
-        load.start()
-
     barrier = pltpu.get_barrier_semaphore()
     for dev in (up, down, sibling, across, pair_x, out_x, pair_z, out_z):
         pl.semaphore_signal(barrier, inc=1, device_id=dev, device_id_type=MESH)
+    for load in loads:
+        load.start()
 
     def screened(h, ref):
         for j in range(2):
@@ -187,10 +189,10 @@
         ref = part_of(s // CHUNKS, far, s % CHUNKS, HALF, HALF)
         return remote(ref, down, fdown_send.at[s], fdown_recv.at[s])
 
-    def to_sibling(s):
+    def to_sibling(s, part):
         return pltpu.make_async_remote_copy(
-            src_ref=sib_out.at[s % CHUNKS], dst_ref=sib_in.at[s],
-            send_sem=sib_send.at[s], recv_sem=sib_recv.at[s],
+            src_ref=sib_out.at[s % CHUNKS, part], dst_ref=sib_in.at[s, part],
+            send_sem=sib_send.at[s * 2 + part], recv_sem=sib_recv.at[s * 2 + part],
             device_id=sibling, device_id_type=MESH,
         )
 
@@ -211,31 +213,39 @@
         from_above(s).wait_recv()
         pass_down(s).start()
 
-    def product(s):
+    def gathered(s):
         far_from_below(s).wait_recv()
         far_from_above(s).wait_recv()
+
+    def product(s, part):
         t, k = s // CHUNKS, s % CHUNKS
+        block = 2 * (zh if part else 1 - zh)
         lhs = jnp.concatenate([amp[t, o, rows_of(k), :] for o in range(RING)], axis=1)
-        for h in range(2):
-            sib_out[k, h] = jnp.dot(
-                lhs, table[h * 2 + (1 - core)], preferred_element_type=jnp.float32
-            )
-        to_sibling(s).start()
-        for h in range(2):
-            own[k, h] = jnp.dot(
-                lhs, table[h * 2 + core], preferred_element_type=jnp.float32
-            )
+        sib_out[k, part] = jnp.dot(
+            lhs, table[block + 1 - core], preferred_element_type=jnp.float32
+        )
+        to_sibling(s, part).start()
+        own[k, part] = jnp.dot(
+            lhs, table[block + core], preferred_element_type=jnp.float32
+        )
+
+    def store(k):
+        rows = rows_of(k)
+        return pltpu.make_async_copy(
+            result.at[rows, :], out_hbm.at[rows, :], stored.at[k]
+        )
 
     def reduce_core(s):
         k = s % CHUNKS
-        to_sibling(s).wait()
-        z_out[k] = (own[k, 1 - zh] + sib_in[s, 1 - zh]).astype(jnp.bfloat16)
+        to_sibling(s, 0).wait()
+        z_out[k] = (own[k, 0] + sib_in[s, 0]).astype(jnp.bfloat16)
         to_across(s).start()
 
     def finish(s):
         t, k = s // CHUNKS, s % CHUNKS
+        to_sibling(s, 1).wait()
         to_across(s).wait()
-        ladder = own[k, zh] + sib_in[s, zh] + z_in[s].astype(jnp.float32)
+        ladder = own[k, 1] + sib_in[s, 1] + z_in[s].astype(jnp.float32)
         value = (coupling_ref[rows_of(k), :] + ladder) * weight[rows_of(k), :]
 
         @pl.when(t < ITERS - 1)
@@ -245,7 +255,8 @@
 
         @pl.when(t == ITERS - 1)
         def _():
-            out_ref[rows_of(k), :] = value
+            result[rows_of(k), :] = value
+            store(k).start()
 
         send_up(s).wait_send()
         send_down(s).wait_send()
@@ -330,18 +341,19 @@
         def _(k):
             forward(k)
 
-    def new_chunk(k):
+    for load in loads[2:]:
+        load.wait()
+
+    @pl.loop(0, CHUNKS)
+    def _(k):
         first_amplitudes(k)
-        start_ring(k)
 
     pl.semaphore_wait(barrier, 8)
     to_swap.start()
     ring_copy(x, None, 0, right).start()
     ring_copy(x, None, 1, left).start()
     over_z(0).start()
-    for load in loads[2:]:
-        load.wait()
-    new_chunk(0)
+    start_ring(0)
 
     to_swap.wait_recv()
     s_first.start()
@@ -353,7 +365,7 @@
 
     @pl.loop(1, CHUNKS // 2)
     def _(k):
-        new_chunk(k)
+        start_ring(k)
 
     ring_copy(x + 3, None, 0, right).wait_recv()
     ring_copy(x + 3, 0, 2, right).start()
@@ -364,7 +376,7 @@
 
     @pl.loop(CHUNKS // 2, CHUNKS)
     def _(k):
-        new_chunk(k)
+        start_ring(k)
 
     forwards(0)
 
@@ -404,15 +416,25 @@
     pl.when(outside)(lambda: s_relay(3))
     forwards(6)
     forwards(7)
+    from_pair = jnp.where(inside, 1 - parity, parity)
+    for n in range(2):
+        arrived(slot_of(core, 1 - zh, n, zl))
+        arrived(s_slots[2 + n](from_pair))
+    gathered(0)
+    product(0, 0)
+    gathered(1)
+    product(1, 0)
+    reduce_core(0)
     for n in range(2):
         arrived(slot_of(core, zh, n, 1 - zl))
-        arrived(slot_of(core, 1 - zh, n, zl))
-    for n in range(4):
-        arrived(s_slots[n](jnp.where(inside, 1 - parity, parity)))
-
-    @pl.loop(0, STEPS + FINAL)
+        arrived(s_slots[n](from_pair))
+
+    def tick_of(tick, lag):
+        return jnp.logical_and(tick >= lag, tick < STEPS + lag)
+
+    @pl.loop(2, STEPS + FINAL)
     def _(tick):
-        @pl.when(jnp.logical_and(tick >= FINAL, tick < STEPS + FINAL))
+        @pl.when(tick_of(tick, FINAL))
         def _():
             finish(tick - FINAL)
 
@@ -420,14 +442,21 @@
         def _():
             forward(tick - FORWARD + CHUNKS)
 
-        @pl.when(jnp.logical_and(tick >= 1, tick < STEPS + 1))
+        @pl.when(tick_of(tick, 1))
         def _():
             reduce_core(tick - 1)
 
         @pl.when(tick < STEPS)
         def _():
-            product(tick)
-
+            gathered(tick)
+            product(tick, 0)
+
+        @pl.when(tick_of(tick, SECOND))
+        def _():
+            product(tick - SECOND, 1)
+
+    for k in range(CHUNKS):
+        store(k).wait()
     to_swap.wait_send()
     for n, (owner, half) in enumerate(((x, None), (x, None), (x + 3, 0), (x + 1, 1))):
         ring_copy(owner, half, n, right).wait_send()
@@ -453,12 +482,11 @@
 def local(coupling, denominators, integrals, tile_sizes, screen_ov, screen_vv):
     dma = pltpu.SemaphoreType.DMA
     anywhere = pl.BlockSpec(memory_space=pl.ANY)
-    vmem = pl.BlockSpec(memory_space=pltpu.VMEM)
     return pl.pallas_call(
         kernel,
         out_shape=jax.ShapeDtypeStruct((ROWS, COLS), jnp.float32),
         in_specs=[anywhere] * 6,
-        out_specs=vmem,
+        out_specs=anywhere,
         scratch_shapes=[
             pltpu.SMEM((32,), jnp.int32),
             pltpu.SMEM((32, 64), jnp.int32),
@@ -467,6 +495,8 @@
             pltpu.VMEM((ROWS, COLS), jnp.float32),
             pltpu.VMEM((COLS, 2 * COLS), jnp.bfloat16),
             dma((6,)),
+            pltpu.VMEM((ROWS, COLS), jnp.float32),
+            dma((CHUNKS,)),
             pltpu.VMEM((ROWS, COLS), jnp.float32),
             pltpu.VMEM((ITERS, RING, ROWS, COLS), jnp.bfloat16),
             pltpu.VMEM((COLS, COLS), jnp.bfloat16),
@@ -479,7 +509,9 @@
             pltpu.VMEM((CHUNKS, CHUNK, COLS), jnp.bfloat16),
             pltpu.VMEM((STEPS, CHUNK, COLS), jnp.bfloat16),
         ]
-        + [dma((STEPS,))] * 12
+        + [dma((STEPS,))] * 8
+        + [dma((2 * STEPS,))] * 2
+        + [dma((STEPS,))] * 2
         + [dma, dma, dma((4,)), dma((4,)), dma((6,)), dma((10,)), dma((16,))],
         compiler_params=pltpu.CompilerParams(
             collective_id=0, has_side_effects=True, vmem_limit_bytes=56 * 1024 * 1024

time: 85.6 us -> 84.3 us (0.985)
  no operation moved by 1% of the time
where the time goes in v4:
time: 84.3 us; the launch traced here: 84.1 us
  Pallas kernels  81.9 us (97%)
  local copies, waits for them, and re-layouts  2.26 us (3%)
    pallas_call x1, Pallas kernels, local(): pl.pallas_call(kernel, out_shape=jax.ShapeDtypeStruct((ROWS, COLS), jnp.f...  81.9 us
    unnamed x1, local copies, waits for them, and re-layouts  2.26 us

profile of v4, /device:TPU:0, one launch (start us, length us, event | category | flops | bytes accessed | tf_op | source)
XLA Modules:
  0.0 84.1 jit_solution(8624711086720325919)
XLA Ops:
  0.0 81.9 %shard_map.64 = f32[1024,256]{1,0:T(8,128)} custom-call(s32[32]{0:T(128)} %sizes_hbm.1, s32[32,64]{1,0:T(8,128)} %bitcast.1, s32[32,32]{1,0:T(8,128)} %vv_hbm.1, f32[1024,256]{1,0:T(8,128)} %coupling_hbm.1, f32[1024,256]{1,0:T(8,128)} %den_hbm.1, bf16[256,512]{1,0:T(8,128)(2,1)} %integrals_hbm.1), custom_call_target="tpu_custom_call" | custom-call | flops 6442450944 | bytes 4194304 | tf_op jit(solution)/shard_map/pallas_call | solution.py:485
  81.9 2.3 %copy.8 = f32[1024,256]{1,0:T(8,128)} copy(f32[1024,256]{1,0:T(8,128)} %shard_map.64) | data formatting | bytes 2097152

commit v5 on v4

--- a/solution.py
+++ b/solution.py
@@ -17,6 +17,7 @@
 SPLIT = ROW_TILE // CHUNK
 STEPS = ITERS * CHUNKS
 HALF = CHUNK // 2
+SCALE_ROWS = 16
 FINAL = 4
 SECOND = 2
 FORWARD = 6
@@ -238,14 +239,23 @@
     def reduce_core(s):
         k = s % CHUNKS
         to_sibling(s, 0).wait()
-        z_out[k] = (own[k, 0] + sib_in[s, 0]).astype(jnp.bfloat16)
+        partial = own[k, 0] + sib_in[s, 0]
+        most = jnp.max(jnp.abs(partial), axis=0, keepdims=True)
+        log = jnp.floor(jnp.log2(jnp.maximum(most, 1e-30)) * 128.0) + 2.0
+        coded = jnp.round(partial * (32766.0 * jnp.exp2(log * (-1.0 / 128.0))))
+        z_out[k, pl.ds(0, CHUNK), :] = coded.astype(jnp.int32).astype(jnp.int16)
+        logs = jnp.broadcast_to(log.astype(jnp.int32), (SCALE_ROWS, COLS))
+        z_out[k, pl.ds(CHUNK, SCALE_ROWS), :] = logs.astype(jnp.int16)
         to_across(s).start()
 
     def finish(s):
         t, k = s // CHUNKS, s % CHUNKS
         to_sibling(s, 1).wait()
         to_across(s).wait()
-        ladder = own[k, 1] + sib_in[s, 1] + z_in[s].astype(jnp.float32)
+        logs = z_in[s, pl.ds(CHUNK, SCALE_ROWS), :].astype(jnp.int32).astype(jnp.float32)
+        scale = jnp.exp2(logs * (1.0 / 128.0))[:1] * (1.0 / 32766.0)
+        coded = z_in[s, pl.ds(0, CHUNK), :].astype(jnp.int32).astype(jnp.float32)
+        ladder = own[k, 1] + sib_in[s, 1] + coded * scale
         value = (coupling_ref[rows_of(k), :] + ladder) * weight[rows_of(k), :]
 
         @pl.when(t < ITERS - 1)
@@ -506,8 +516,8 @@
             pltpu.VMEM((CHUNKS, 2, CHUNK, COLS), jnp.float32),
             pltpu.VMEM((CHUNKS, 2, CHUNK, COLS), jnp.float32),
             pltpu.VMEM((STEPS, 2, CHUNK, COLS), jnp.float32),
-            pltpu.VMEM((CHUNKS, CHUNK, COLS), jnp.bfloat16),
-            pltpu.VMEM((STEPS, CHUNK, COLS), jnp.bfloat16),
+            pltpu.VMEM((CHUNKS, CHUNK + SCALE_ROWS, COLS), jnp.int16),
+            pltpu.VMEM((STEPS, CHUNK + SCALE_ROWS, COLS), jnp.int16),
         ]
         + [dma((STEPS,))] * 8
         + [dma((2 * STEPS,))] * 2

time: 84.3 us -> 85.2 us (1.011)
    pallas_call x1, Pallas kernels: 81.9 us -> 82.7 us  [local(): pl.pallas_call(kernel, out_shape=jax.ShapeDtypeStruct((ROWS, COLS), jnp.f...]
where the time goes in v5:
time: 85.2 us; the launch traced here: 85 us
  Pallas kernels  82.7 us (97%)
  local copies, waits for them, and re-layouts  2.26 us (3%)
    pallas_call x1, Pallas kernels, local(): pl.pallas_call(kernel, out_shape=jax.ShapeDtypeStruct((ROWS, COLS), jnp.f...  82.7 us
    unnamed x1, local copies, waits for them, and re-layouts  2.26 us

profile of v5, /device:TPU:0, one launch (start us, length us, event | category | flops | bytes accessed | tf_op | source)
XLA Modules:
  0.0 85.0 jit_solution(15249121252952927539)
XLA Ops:
  0.0 82.7 %shard_map.64 = f32[1024,256]{1,0:T(8,128)} custom-call(s32[32]{0:T(128)} %sizes_hbm.1, s32[32,64]{1,0:T(8,128)} %bitcast.1, s32[32,32]{1,0:T(8,128)} %vv_hbm.1, f32[1024,256]{1,0:T(8,128)} %coupling_hbm.1, f32[1024,256]{1,0:T(8,128)} %den_hbm.1, bf16[256,512]{1,0:T(8,128)(2,1)} %integrals_hbm.1), custom_call_target="tpu_custom_call" | custom-call | flops 6442450944 | bytes 4194304 | tf_op jit(solution)/shard_map/pallas_call | solution.py:495
  82.7 2.3 %copy.8 = f32[1024,256]{1,0:T(8,128)} copy(f32[1024,256]{1,0:T(8,128)} %shard_map.64) | data formatting | bytes 2097152

commit v6 on v5

--- a/solution.py
+++ b/solution.py
@@ -420,12 +420,15 @@
 
     pl.when(outside)(lambda: s_relay(2))
     for n in range(2):
-        arrived(slot_of(core, 1 - zh, n, 1 - zl))
-        o_pass(n).start()
-        forwards(4 + n)
+        which = (parity + n) % 2
+        arrived(slot_of(core, 1 - zh, which, 1 - zl))
+        o_pass(which).start()
     pl.when(outside)(lambda: s_relay(3))
-    forwards(6)
-    forwards(7)
+
+    @pl.loop(4, CHUNKS)
+    def _(k):
+        forward(k)
+
     from_pair = jnp.where(inside, 1 - parity, parity)
     for n in range(2):
         arrived(slot_of(core, 1 - zh, n, zl))
@@ -448,13 +451,13 @@
         def _():
             finish(tick - FINAL)
 
+        @pl.when(tick_of(tick, 1))
+        def _():
+            reduce_core(tick - 1)
+
         @pl.when(jnp.logical_and(tick >= FORWARD, tick < STEPS - CHUNKS + FORWARD))
         def _():
             forward(tick - FORWARD + CHUNKS)
-
-        @pl.when(tick_of(tick, 1))
-        def _():
-            reduce_core(tick - 1)
 
         @pl.when(tick < STEPS)
         def _():

time: 85.2 us -> 85 us (level)
  no operation moved by 1% of the time
where the time goes in v6:
time: 85 us; the launch traced here: 84.8 us
  Pallas kernels  82.5 us (97%)
  local copies, waits for them, and re-layouts  2.26 us (3%)
    pallas_call x1, Pallas kernels, local(): pl.pallas_call(kernel, out_shape=jax.ShapeDtypeStruct((ROWS, COLS), jnp.f...  82.5 us
    unnamed x1, local copies, waits for them, and re-layouts  2.26 us

profile of v6, /device:TPU:0, one launch (start us, length us, event | category | flops | bytes accessed | tf_op | source)
XLA Modules:
  0.0 84.8 jit_solution(4709296594945039759)
XLA Ops:
  0.0 82.5 %shard_map.64 = f32[1024,256]{1,0:T(8,128)} custom-call(s32[32]{0:T(128)} %sizes_hbm.1, s32[32,64]{1,0:T(8,128)} %bitcast.1, s32[32,32]{1,0:T(8,128)} %vv_hbm.1, f32[1024,256]{1,0:T(8,128)} %coupling_hbm.1, f32[1024,256]{1,0:T(8,128)} %den_hbm.1, bf16[256,512]{1,0:T(8,128)(2,1)} %integrals_hbm.1), custom_call_target="tpu_custom_call" | custom-call | flops 6442450944 | bytes 4194304 | tf_op jit(solution)/shard_map/pallas_call | solution.py:498
  82.5 2.3 %copy.8 = f32[1024,256]{1,0:T(8,128)} copy(f32[1024,256]{1,0:T(8,128)} %shard_map.64) | data formatting | bytes 2097152
